TPU v7x, 256 devices: a whole 4x4x8 slice. The times are simulated.
256 devices in a mesh: lang: 8 (over z), shard: 32 (over y, x, core).
Axes of the slice: x: 4, y: 4, z: 8, core: 2. Of those that a mesh axis runs over, the one named last changes fastest.
Arguments:
- memory: bfloat16 [256, 16, 4096], P(('lang', 'shard')), may hold values from -6 to 6
- lang_id: int32 [256], P(('lang', 'shard')), may hold values from 0 to 7, as said below
- src_len: int32 [256], P(('lang', 'shard')), may hold values from 4 to 16
- tgt_len: int32 [256], P(('lang', 'shard')), may hold values from 32 to 128
- queries: bfloat16 [8, 64, 128, 4096], P('lang', 'shard'), may hold values from -64 to 64
- key_weight: bfloat16 [8, 4096, 4096], P('lang', None, 'shard'), may hold values from -1 to 1
- value_weight: bfloat16 [8, 4096, 4096], P('lang', None, 'shard'), may hold values from -0.09375 to 0.09375
- grad_context: bfloat16 [8, 64, 128, 4096], P('lang', 'shard'), may hold values from -6 to 6
Outputs:
- context: bfloat16 [8, 64, 128, 4096], P('lang', 'shard')
- grad_queries: bfloat16 [8, 64, 128, 4096], P('lang', 'shard')
- grad_memory: bfloat16 [256, 16, 4096], P(('lang', 'shard'))
- grad_key_weight: bfloat16 [8, 4096, 4096], P('lang', None, 'shard')
- grad_value_weight: bfloat16 [8, 4096, 4096], P('lang', None, 'shard')
Inputs may be any that keep to these rules, and one draw needn't show every extreme that they name: `lang_id`: among the 8 sentences of one column b (indices a * 32 + b), no language is named more than 2 times, and in every column some language is named exactly 2 times.
All inputs are finite; a program needn't handle non-finite values.
Results may differ from a plain program's by a relative error of at most 0.025.
The roundings to bfloat16 on the way count: a program that leaves them out, or rounds other values in their place, can miss the bound.
Values may be sent and summed in bfloat16 or wider, within the bound.
No kernel may reach another device: no remote copies, remote signals or barrier semaphores. Data moves between devices by JAX's collectives and lax.ppermute only.
A program may use at most 128 MiB of HBM per device.

v0:
```python
import jax
import jax.numpy as jnp
from jax import lax
from jax.sharding import PartitionSpec as P

HEAD = 128
masked_score = -1e30


def attend(queries, key_rows, value_rows, grad_ctx, src_slot, tgt_slot):
    scaling = queries.shape[-1] ** (-0.5)
    source_rows = key_rows.shape[1]
    target_rows = queries.shape[1]
    scores = (
        jnp.einsum("nqhe,nkhe->nhqk", queries, key_rows, preferred_element_type=jnp.float32)
        * scaling
    )
    key_valid = jnp.arange(source_rows)[None, :] < jnp.maximum(src_slot, 1)[:, None]
    scores = jnp.where(key_valid[:, None, None, :], scores, masked_score)
    row_max = jnp.max(scores, axis=-1, keepdims=True)
    shifted = jnp.exp(scores - row_max)
    attention = shifted / jnp.sum(shifted, axis=-1, keepdims=True)
    attention_bf = attention.astype(jnp.bfloat16)
    row_valid = (jnp.arange(target_rows)[None, :] < tgt_slot[:, None])[:, :, None, None]
    context = jnp.einsum(
        "nhqk,nkhe->nqhe", attention_bf, value_rows, preferred_element_type=jnp.float32
    )
    context = jnp.where(row_valid, context, 0.0).astype(jnp.bfloat16)
    grad_masked = jnp.where(row_valid, grad_ctx, jnp.zeros_like(grad_ctx))
    grad_values = jnp.einsum(
        "nhqk,nqhe->nkhe", attention_bf, grad_masked, preferred_element_type=jnp.float32
    ).astype(jnp.bfloat16)
    grad_attention = jnp.einsum(
        "nqhe,nkhe->nhqk", grad_masked, value_rows, preferred_element_type=jnp.float32
    )
    row_dot = jnp.sum(attention * grad_attention, axis=-1, keepdims=True)
    grad_scores = (attention * (grad_attention - row_dot)).astype(jnp.bfloat16)
    grad_queries = (
        jnp.einsum("nhqk,nkhe->nqhe", grad_scores, key_rows, preferred_element_type=jnp.float32)
        * scaling
    ).astype(jnp.bfloat16)
    grad_keys = (
        jnp.einsum("nhqk,nqhe->nkhe", grad_scores, queries, preferred_element_type=jnp.float32)
        * scaling
    ).astype(jnp.bfloat16)
    return (context, grad_queries, grad_keys, grad_values)


def local(memory, lang_id, src_len, tgt_len, queries, key_weight, value_weight, grad_context):
    lang_count = lax.axis_size("lang")
    shard_count = lax.axis_size("shard")
    lang_index = lax.axis_index("lang")
    column_mem, column_ids, column_src, column_tgt = (
        lax.all_gather(memory, "lang", axis=0, tiled=True),
        lax.all_gather(lang_id, "lang", axis=0, tiled=True),
        lax.all_gather(src_len, "lang", axis=0, tiled=True),
        lax.all_gather(tgt_len, "lang", axis=0, tiled=True),
    )
    slots_dev = queries.shape[1]
    target_rows = queries.shape[2]
    source_rows = memory.shape[1]
    model_width = memory.shape[2]
    head_cols = key_weight.shape[2]
    matching = column_ids[:, None] == column_ids[None, :]
    earlier = jnp.arange(lang_count)[None, :] < jnp.arange(lang_count)[:, None]
    position = jnp.sum(jnp.where(matching & earlier, 1, 0), axis=1).astype(jnp.int32)
    selected = (column_ids[None, :] == lang_index) & (
        position[None, :] == jnp.arange(slots_dev)[:, None]
    )
    routed = jnp.einsum(
        "rj,jsd->rsd", selected.astype(jnp.bfloat16), column_mem, preferred_element_type=jnp.float32
    ).astype(jnp.bfloat16)
    own_src = jnp.sum(jnp.where(selected, column_src[None, :], 0), axis=1).astype(jnp.int32)
    own_tgt = jnp.sum(jnp.where(selected, column_tgt[None, :], 0), axis=1).astype(jnp.int32)
    key_local = key_weight[0]
    value_local = value_weight[0]
    group_rows = lax.all_gather(routed, "shard", axis=0, tiled=True)
    flattened = group_rows.reshape(-1, model_width)
    key_part = jnp.dot(flattened, key_local, preferred_element_type=jnp.float32).astype(
        jnp.bfloat16
    )
    value_part = jnp.dot(flattened, value_local, preferred_element_type=jnp.float32).astype(
        jnp.bfloat16
    )
    joined = jnp.concatenate([key_part, value_part], axis=1)
    projected = joined.reshape(group_rows.shape[0], source_rows, 2 * head_cols)
    key_rows = projected[:, :, :head_cols]
    value_rows = projected[:, :, head_cols:]
    total_slots = key_rows.shape[0]
    local_heads = head_cols // HEAD
    src_all, tgt_all = (
        lax.all_gather(own_src, "shard", axis=0, tiled=True),
        lax.all_gather(own_tgt, "shard", axis=0, tiled=True),
    )
    query_split = queries[0].reshape(slots_dev, target_rows, shard_count, head_cols)
    grad_split = grad_context[0].reshape(slots_dev, target_rows, shard_count, head_cols)
    query_heads, grad_heads = (
        lax.all_to_all(query_split, "shard", split_axis=2, concat_axis=0, tiled=True),
        lax.all_to_all(grad_split, "shard", split_axis=2, concat_axis=0, tiled=True),
    )
    source_shape = (total_slots, source_rows, local_heads, HEAD)
    context_heads, grad_query_heads, grad_keys, grad_values = attend(
        query_heads,
        key_rows.reshape(source_shape),
        value_rows.reshape(source_shape),
        grad_heads,
        src_all,
        tgt_all,
    )
    outgoing = (context_heads, grad_query_heads)
    context_slots, grad_query_slots = (
        lax.all_to_all(outgoing[0], "shard", split_axis=0, concat_axis=2, tiled=True),
        lax.all_to_all(outgoing[1], "shard", split_axis=0, concat_axis=2, tiled=True),
    )
    context = context_slots.reshape(1, slots_dev, target_rows, shard_count * head_cols)
    grad_queries = grad_query_slots.reshape(1, slots_dev, target_rows, shard_count * head_cols)
    grad_keys = grad_keys.reshape(total_slots, source_rows, head_cols)
    grad_values = grad_values.reshape(total_slots, source_rows, head_cols)
    key_part = grad_keys.reshape(-1, head_cols)
    value_part = grad_values.reshape(-1, head_cols)
    contract = (((1,), (1,)), ((), ()))
    summed = lax.dot_general(key_part, key_local, contract, preferred_element_type=jnp.float32)
    summed = summed + lax.dot_general(
        value_part, value_local, contract, preferred_element_type=jnp.float32
    )
    slot_grads = lax.psum_scatter(
        summed.reshape(lax.axis_size("shard") * slots_dev, source_rows, model_width).astype(
            jnp.bfloat16
        ),
        "shard",
        scatter_dimension=0,
        tiled=True,
    )
    transpose_contract = (((0,), (0,)), ((), ()))
    flattened = group_rows.reshape(-1, model_width)
    grad_key_local = lax.dot_general(
        flattened,
        grad_keys.reshape(-1, head_cols),
        transpose_contract,
        preferred_element_type=jnp.float32,
    )
    grad_value_local = lax.dot_general(
        flattened,
        grad_values.reshape(-1, head_cols),
        transpose_contract,
        preferred_element_type=jnp.float32,
    )
    returned = lax.all_gather(slot_grads, "lang", axis=0, tiled=True)
    own_index = lang_id[0] * slots_dev + position[lang_index]
    grad_memory = lax.dynamic_slice_in_dim(returned, own_index, 1, 0)
    return (
        context,
        grad_queries,
        grad_memory,
        grad_key_local.astype(jnp.bfloat16)[None],
        grad_value_local.astype(jnp.bfloat16)[None],
    )


def solution(mesh):
    return jax.shard_map(
        local,
        mesh=mesh,
        in_specs=(
            P(("lang", "shard"), None, None),
            P(("lang", "shard")),
            P(("lang", "shard")),
            P(("lang", "shard")),
            P("lang", "shard", None, None),
            P("lang", None, "shard"),
            P("lang", None, "shard"),
            P("lang", "shard", None, None),
        ),
        out_specs=(
            P("lang", "shard", None, None),
            P("lang", "shard", None, None),
            P(("lang", "shard"), None, None),
            P("lang", None, "shard"),
            P("lang", None, "shard"),
        ),
        check_vma=False,
    )
```

profile of v0, /device:TPU:32, one launch (start us, length us, event | category | flops | bytes accessed | tf_op | source)
XLA Modules:
  0.0 345.6 jit_solution(13995606960444535053)
XLA Ops:
  7.2 0.0 copy-start
  7.2 0.0 all-gather.4.cloned.1.call-start
  7.2 0.7 all-gather.4.cloned.1.call-update
  7.9 0.0 all-gather.6.cloned.1.call-start
  9.9 1.3 dynamic-slice
  11.2 0.8 dynamic-update-slice
  11.9 0.8 dynamic-update-slice.3
  12.7 0.8 dynamic-update-slice.1
  13.4 15.2 %all-reduce.6 = (s32[8]{0:T(128)S(1)}, s32[8]{0:T(128)S(1)}, s32[8]{0:T(128)S(1)}) all-reduce(s32[8]{0:T(128)S(1)} %dynamic-update-slice.3, s32[8]{0:T(128)S(1)} %dynamic-update-slice, s32[8]{0:T(128)S(1)} %dynamic-update-slice.1), channel_id=1, replica_groups=mesh['lang'=8,'shard'=32] {'lang'}, use_global_device_ids=true, to_apply=%add.3 | all-reduce | flops 24 | bytes 192
  28.7 0.2 select_reduce_fusion
  28.8 21.6 %all-gather.4.cloned.1.call-done = bf16[8,16,4096]{2,1,0:T(8,128)(2,1)} async-done(((bf16[1,16,4096]{2,1,0:T(8,128)(2,1)}), bf16[8,16,4096]{2,1,0:T(8,128)(2,1)}) %all-gather.4.cloned.1.call-update) | async-done | bytes 1048592 | tf_op jit(solution)/shard_map/all_gather | solution.py:54
  50.5 2.5 convolution_convert_fusion.2
  53.0 0.9 copy.46
  53.9 0.0 all-gather.6.cloned.1.call-update
  53.9 3.1 copy.51
  57.0 2.7 copy.52
  59.8 7.1 %all-to-all-start.2 = ((bf16[2,128,32,128]{3,1,0,2:T(8,128)(2,1)}), bf16[2,128,32,128]{3,1,0,2:T(8,128)(2,1)S(1)}, u32[]{:S(2)}, u32[]{:S(2)}) async-start(bf16[2,128,32,128]{3,1,0,2:T(8,128)(2,1)} %copy.52), calls=%async_computation.2 | async-start | bytes 4194304 | tf_op jit(solution)/shard_map/all_to_all | solution.py:99
  66.9 0.6 dynamic-slice.2
  67.5 2.1 copy.55
  69.5 2.1 copy.48
  72.3 0.1 select_reduce_fusion.1
  72.5 0.2 dynamic-update-slice.2
  72.7 0.2 dynamic-update-slice.4
  72.9 33.9 %all-reduce.5 = (s32[64]{0:T(128)S(1)}, s32[64]{0:T(128)S(1)}) all-reduce(s32[64]{0:T(128)S(1)} %dynamic-update-slice.2, s32[64]{0:T(128)S(1)} %dynamic-update-slice.4), channel_id=1, replica_groups=mesh['lang'=8,'shard'=32] {'shard'}, use_global_device_ids=true, to_apply=%add.2 | all-reduce | flops 128 | bytes 1024
  106.9 0.1 iota_compare_fusion.1
  107.0 1.3 copy-done.3
  108.3 4.0 %all-to-all-start = ((bf16[2,128,32,128]{3,1,0,2:T(8,128)(2,1)}), bf16[2,128,32,128]{3,1,0,2:T(8,128)(2,1)S(1)}, u32[]{:S(2)}, u32[]{:S(2)}) async-start(bf16[2,128,32,128]{3,1,0,2:T(8,128)(2,1)} %copy.48), calls=%async_computation | async-start | bytes 4194304 | tf_op jit(solution)/shard_map/all_to_all | solution.py:98
  112.3 0.0 reduce-scatter.2.cloned.1.call-start
  112.3 0.1 iota_compare_fusion
  112.4 4.5 %bitcast_select_fusion.1 = bf16[64,128,128]{2,1,0:T(8,128)(2,1)} fusion(bf16[2,128,32,128]{3,1,0,2:T(8,128)(2,1)} %copy-done.3, pred[64,128]{1,0:T(8,128)(4,1)S(1)} %iota_compare_fusion.1), kind=kLoop, calls=%fused_computation.10 | loop fusion | flops 1048576 | bytes 4202496 | tf_op jit(solution)/shard_map/jit(_where)/select_n | solution.py:29
  116.9 33.4 %all-gather.6.cloned.1.call-done = bf16[64,16,4096]{2,1,0:T(8,128)(2,1)} async-done(((bf16[2,16,4096]{2,1,0:T(8,128)(2,1)}), bf16[64,16,4096]{2,1,0:T(8,128)(2,1)}) %all-gather.6.cloned.1.call-update) | async-done | bytes 8388624 | tf_op jit(solution)/shard_map/all_gather | solution.py:77
  150.4 6.7 %convolution_convert_fusion.4 = bf16[1024,128]{0,1:T(8,128)(2,1)S(1)} fusion(bf16[1024,4096]{1,0:T(8,128)(2,1)} %bitcast.101, bf16[1,4096,128]{2,1,0:T(8,128)(2,1)} %param.14), kind=kOutput, calls=%fused_computation.20 | convolution fusion | flops 1073872896 | bytes 9699328 | tf_op jit(solution)/shard_map/dot_general | solution.py:82
  157.1 2.9 convolution_convert_fusion.5
  160.0 0.8 pad_maximum_fusion
  160.8 2.0 copy.47
  162.8 2.1 fusion.9
  165.0 0.8 copy-done.7
  165.8 0.9 fusion.26
  166.7 3.3 convolution_convert_fusion.3
  170.0 3.0 multiply_reduce_fusion
  173.0 0.0 copy-done.5
  173.0 0.1 multiply_convert_fusion.1
  173.1 0.7 fusion.10
  173.8 8.1 %fusion.13 = f32[1024,4096]{1,0:T(8,128)} fusion(bf16[1024,128]{1,0:T(8,128)(2,1)S(1)} %bitcast.116, bf16[1,4096,128]{2,1,0:T(8,128)(2,1)S(1)} %copy-done), kind=kOutput, calls=%fused_computation.25 | convolution fusion | flops 1073741824 | bytes 18087936 | tf_op jit(solution)/shard_map/dot_general | solution.py:122
  181.9 11.4 %add_convert_fusion = bf16[1024,4096]{1,0:T(8,128)(2,1)} fusion(f32[1024,4096]{1,0:T(8,128)} %fusion.13, bf16[1024,128]{1,0:T(8,128)(2,1)S(1)} %bitcast.118, bf16[1,4096,128]{2,1,0:T(8,128)(2,1)S(1)} %copy-done.4), kind=kOutput, calls=%fused_computation.1 | convolution fusion | flops 1082130432 | bytes 26476544 | tf_op jit(solution)/shard_map/dot_general | solution.py:123
  193.3 0.0 reduce-scatter.2.cloned.1.call-update
  193.3 1.0 copy-done.6
  194.4 0.2 copy-done.8
  194.5 2.4 fusion.5
  196.9 6.1 %all-to-all-start.1 = ((bf16[64,128,1,128]{1,3,2,0:T(8,128)(2,1)}), bf16[64,128,1,128]{1,3,2,0:T(8,128)(2,1)S(1)}, u32[]{:S(2)}, u32[]{:S(2)}) async-start(bf16[64,128,1,128]{1,3,2,0:T(8,128)(2,1)} %fusion.5), calls=%async_computation.1 | async-start | bytes 4194304 | tf_op jit(solution)/shard_map/all_to_all | solution.py:112
  203.0 0.0 all-gather.8.cloned.1.call-start
  203.1 91.0 %reduce-scatter.2.cloned.1.call-done = bf16[2,16,4096]{2,1,0:T(8,128)(2,1)} async-done(((bf16[64,16,4096]{2,1,0:T(8,128)(2,1)}), bf16[2,16,4096]{2,1,0:T(8,128)(2,1)}) %reduce-scatter.2.cloned.1.call-update) | async-done | bytes 262160 | tf_op jit(solution)/shard_map/reduce_scatter | solution.py:126
  294.1 0.0 all-gather.8.cloned.1.call-update
  294.1 2.1 fusion.4
  296.2 5.5 %all-to-all-start.3 = ((bf16[64,128,1,128]{1,3,2,0:T(8,128)(2,1)}), bf16[64,128,1,128]{1,3,2,0:T(8,128)(2,1)}, u32[]{:S(2)}, u32[]{:S(2)}) async-start(bf16[64,128,1,128]{1,3,2,0:T(8,128)(2,1)} %fusion.4), calls=%async_computation.3 | async-start | bytes 4194304 | tf_op jit(solution)/shard_map/all_to_all | solution.py:113
  301.7 0.6 dynamic_slice.6
  303.0 6.8 %fusion.1 = bf16[1,4096,128]{2,1,0:T(8,128)(2,1)} fusion(bf16[1024,4096]{1,0:T(8,128)(2,1)} %bitcast.102, bf16[1024,128]{1,0:T(8,128)(2,1)S(1)} %bitcast.117), kind=kOutput, calls=%fused_computation.4 | convolution fusion | flops 1074266112 | bytes 9699328 | tf_op jit(solution)/shard_map/dot_general | solution.py:136
  309.8 6.8 %fusion.2 = bf16[1,4096,128]{2,1,0:T(8,128)(2,1)} fusion(bf16[1024,4096]{1,0:T(8,128)(2,1)} %bitcast.103, bf16[1024,128]{1,0:T(8,128)(2,1)S(1)} %bitcast.119), kind=kOutput, calls=%fused_computation.5 | convolution fusion | flops 1074266112 | bytes 9699328 | tf_op jit(solution)/shard_map/dot_general | solution.py:142
  316.6 2.9 copy.50
  319.5 4.2 %reshape.151 = bf16[1,2,128,4096]{3,2,1,0:T(8,128)(2,1)} reshape(bf16[2,128,32,1,128]{4,2,1,0,3:T(8,128)(2,1)} %copy.50) | data formatting | bytes 4194304 | tf_op jit(solution)/shard_map/reshape | solution.py:115
  323.6 8.0 %all-to-all-done.3 = bf16[64,128,1,128]{1,3,2,0:T(8,128)(2,1)} async-done(((bf16[64,128,1,128]{1,3,2,0:T(8,128)(2,1)}), bf16[64,128,1,128]{1,3,2,0:T(8,128)(2,1)}, u32[]{:S(2)}, u32[]{:S(2)}) %all-to-all-start.3) | async-done | bytes 2097184 | tf_op jit(solution)/shard_map/all_to_all | solution.py:113
  331.7 3.6 %copy.54 = bf16[2,128,32,1,128]{4,2,1,0,3:T(8,128)(2,1)S(1)} copy(bf16[2,128,32,1,128]{1,4,0,2,3:T(8,128)(2,1)} %bitcast.24) | data formatting | bytes 4194304 | tf_op jit(solution)/shard_map/all_to_all | solution.py:113
  335.2 2.3 reshape.152
  337.5 1.6 constant_dynamic-slice_fusion
  (33 shorter events, 0.1 us)
Async XLA Ops:
  7.2 149.9 %copy-start = (bf16[1,4096,128]{2,1,0:T(8,128)(2,1)S(1)}, bf16[1,4096,128]{2,1,0:T(8,128)(2,1)}, u32[]{:S(2)}) copy-start(bf16[1,4096,128]{2,1,0:T(8,128)(2,1)} %param.13) | copy-start | bytes 3145732
  7.2 43.3 %all-gather.4.cloned.1.call-start = ((), (), s32[]{:S(2)}) async-start(), calls=%async_computation.5 | async-start | bytes 1179648 | tf_op jit(solution)/shard_map/all_gather | solution.py:54
  7.9 142.5 %all-gather.6.cloned.1.call-start = ((), (), s32[]{:S(2)}) async-start(), calls=%async_computation.6 | async-start | bytes 8650752 | tf_op jit(solution)/shard_map/all_gather | solution.py:77
  59.8 7.1 %copy-start.13 = (u32[256]{0:T(256)S(1)}, u32[256]{0:T(256)}, u32[]{:S(2)}) copy-start(u32[256]{0:T(256)} %constant.50) | copy-start | bytes 3076
  59.8 47.2 %all-to-all-start.2 = ((bf16[2,128,32,128]{3,1,0,2:T(8,128)(2,1)}), bf16[2,128,32,128]{3,1,0,2:T(8,128)(2,1)S(1)}, u32[]{:S(2)}, u32[]{:S(2)}) async-start(bf16[2,128,32,128]{3,1,0,2:T(8,128)(2,1)} %copy.52), calls=%async_computation.2 | async-start | bytes 4194304 | tf_op jit(solution)/shard_map/all_to_all | solution.py:99
  106.9 1.3 copy-start.3
  108.3 54.6 %all-to-all-start = ((bf16[2,128,32,128]{3,1,0,2:T(8,128)(2,1)}), bf16[2,128,32,128]{3,1,0,2:T(8,128)(2,1)S(1)}, u32[]{:S(2)}, u32[]{:S(2)}) async-start(bf16[2,128,32,128]{3,1,0,2:T(8,128)(2,1)} %copy.48), calls=%async_computation | async-start | bytes 4194304 | tf_op jit(solution)/shard_map/all_to_all | solution.py:98
  112.3 181.8 %reduce-scatter.2.cloned.1.call-start = ((), (), s32[]{:S(2)}) async-start(), calls=%async_computation.7 | async-start | bytes 8650752 | tf_op jit(solution)/shard_map/reduce_scatter | solution.py:126
  150.4 6.7 %copy-start.2 = (bf16[64,16,4096]{2,1,0:T(8,128)(2,1)S(1)}, bf16[64,16,4096]{2,1,0:T(8,128)(2,1)}, u32[]{:S(2)}) copy-start(bf16[64,16,4096]{2,1,0:T(8,128)(2,1)} %all-gather.6.cloned.1.call-done) | copy-start | bytes 25165828
  165.0 0.8 copy-start.7
  170.0 3.0 copy-start.5
  173.8 8.1 %copy-start.9 = (bf16[64,16,128]{2,1,0:T(8,128)(2,1)}, bf16[64,16,128]{2,1,0:T(8,128)(2,1)S(1)}, u32[]{:S(2)}) copy-start(bf16[64,16,128]{2,1,0:T(8,128)(2,1)S(1)} %fusion.10) | copy-start | bytes 786436
  173.8 8.1 %copy-start.4 = (bf16[1,4096,128]{2,1,0:T(8,128)(2,1)S(1)}, bf16[1,4096,128]{2,1,0:T(8,128)(2,1)}, u32[]{:S(2)}) copy-start(bf16[1,4096,128]{2,1,0:T(8,128)(2,1)} %param.14) | copy-start | bytes 3145732
  173.8 8.1 %copy-start.11 = (bf16[64,128,16]{1,2,0:T(8,128)(2,1)S(1)}, bf16[64,128,16]{1,2,0:T(8,128)(2,1)}, u32[]{:S(2)}) copy-start(bf16[64,128,16]{1,2,0:T(8,128)(2,1)} %convolution_convert_fusion.3) | copy-start | bytes 786436
  193.3 1.0 copy-start.6
  193.3 1.2 copy-start.8
  196.9 99.2 %all-to-all-start.1 = ((bf16[64,128,1,128]{1,3,2,0:T(8,128)(2,1)}), bf16[64,128,1,128]{1,3,2,0:T(8,128)(2,1)S(1)}, u32[]{:S(2)}, u32[]{:S(2)}) async-start(bf16[64,128,1,128]{1,3,2,0:T(8,128)(2,1)} %fusion.5), calls=%async_computation.1 | async-start | bytes 4194304 | tf_op jit(solution)/shard_map/all_to_all | solution.py:112
  203.0 134.5 %all-gather.8.cloned.1.call-start = ((), (), s32[]{:S(2)}) async-start(), calls=%async_computation.8 | async-start | bytes 2359296 | tf_op jit(solution)/shard_map/all_gather | solution.py:148
  296.2 6.8 %copy-start.10 = (bf16[64,16,128]{2,1,0:T(8,128)(2,1)S(1)}, bf16[64,16,128]{2,1,0:T(8,128)(2,1)}, u32[]{:S(2)}) copy-start(bf16[64,16,128]{2,1,0:T(8,128)(2,1)} %copy-done.9) | copy-start | bytes 786436
  296.2 35.5 %all-to-all-start.3 = ((bf16[64,128,1,128]{1,3,2,0:T(8,128)(2,1)}), bf16[64,128,1,128]{1,3,2,0:T(8,128)(2,1)}, u32[]{:S(2)}, u32[]{:S(2)}) async-start(bf16[64,128,1,128]{1,3,2,0:T(8,128)(2,1)} %fusion.4), calls=%async_computation.3 | async-start | bytes 4194304 | tf_op jit(solution)/shard_map/all_to_all | solution.py:113
  302.9 6.8 %copy-start.12 = (bf16[64,128,16]{1,2,0:T(8,128)(2,1)S(1)}, bf16[64,128,16]{1,2,0:T(8,128)(2,1)}, u32[]{:S(2)}) copy-start(bf16[64,128,16]{1,2,0:T(8,128)(2,1)} %convolution_convert_fusion.3) | copy-start | bytes 786436
  331.7 7.4 %copy-start.1 = (bf16[1,4096,128]{2,1,0:T(8,128)(2,1)S(1)}, bf16[1,4096,128]{2,1,0:T(8,128)(2,1)}, u32[]{:S(2)}) copy-start(bf16[1,4096,128]{2,1,0:T(8,128)(2,1)} %param.13) | copy-start | bytes 3145732
Sparse Core Ops, SparseCore 0:
  9.8 40.6 all-gather.3
  54.0 96.3 all-gather.5
  193.5 100.5 reduce-scatter.1
  295.8 40.1 all-gather.7
where the time goes:
time: 347 us; the launch traced here: 346 us
  waiting for transfers between devices  155 us (45%)
  matrix products  58.8 us (17%)
  blocking collectives  49.1 us (14%)
  local copies, waits for them, and re-layouts  35.9 us (10%)
  starting transfers between devices  22.8 us (7%)
  between operations  17.2 us (5%)
  other arithmetic  6.87 us (2%)
    reduce_scatter x1, waiting for transfers between devices, local(): lax.psum_scatter(summed.reshape(lax.axis_size('shard') * slots_dev, sourc...  91 us
    unnamed x2, blocking collectives  49.1 us
    all_gather x1, waiting for transfers between devices, local(): group_rows = lax.all_gather(routed, 'shard', axis=0, tiled=True)  33.4 us
    all_gather x1, waiting for transfers between devices, local(): lax.all_gather(memory, 'lang', axis=0, tiled=True)  21.6 us
    unnamed x42, local copies, waits for them, and re-layouts  13.1 us
    dot_general x1, matrix products, local(): lax.dot_general(value_part, value_local, contract, preferred_element_type...  11.4 us
    dot_general x1, matrix products, local(): lax.dot_general(key_part, key_local, contract, preferred_element_type=jnp...  8.08 us
    all_to_all x1, waiting for transfers between devices, local(): lax.all_to_all(outgoing[1], 'shard', split_axis=0, concat_axis=2, tiled=T...  8.02 us
  transfers between devices with their start and end apart: 8, of which 4 were waited for; matrix products, arithmetic and copies ran while one was open for 18% of the time, Pallas kernels for 0%

commit v1 on v0

--- a/solution.py
+++ b/solution.py
@@ -74,7 +74,9 @@
     own_tgt = jnp.sum(jnp.where(selected, column_tgt[None, :], 0), axis=1).astype(jnp.int32)
     key_local = key_weight[0]
     value_local = value_weight[0]
-    group_rows = lax.all_gather(routed, "shard", axis=0, tiled=True)
+    group_rows = jnp.concatenate(
+        lax.all_to_all(jnp.stack([routed] * lax.axis_size("shard")), "shard", 0, 0), axis=0
+    )
     flattened = group_rows.reshape(-1, model_width)
     key_part = jnp.dot(flattened, key_local, preferred_element_type=jnp.float32).astype(
         jnp.bfloat16

time: 347 us -> 390 us (1.12)
  blocking collectives: 49.1 us -> 121 us
  waiting for transfers between devices: 155 us -> 116 us
  starting transfers between devices: 22.8 us -> 29.5 us
    unnamed x2, blocking collectives: 49.1 us -> 121 us
    all_gather x1 -> x0, waiting for transfers between devices: 33.4 us -> none  [local(): group_rows = lax.all_gather(routed, 'shard', axis=0, tiled=True)]
    all_gather x1, waiting for transfers between devices: 21.6 us -> 9.03 us  [local(): lax.all_gather(memory, 'lang', axis=0, tiled=True)]
    all_to_all x1, waiting for transfers between devices: 0.01 us -> 9.91 us  [local(): lax.all_to_all(query_split, 'shard', split_axis=2, concat_axis=0, tiled=T...]
    all_to_all x0 -> x1, starting transfers between devices: none -> 7.35 us  [local(): lax.all_to_all(jnp.stack([routed] * lax.axis_size('shard')), 'shard', 0, 0)]
    another operation x0 -> x1, local copies, waits for them, and re-layouts: none -> 4.27 us  [local(): jnp.stack([routed] * lax.axis_size('shard'))]
    unnamed x42 -> x44, local copies, waits for them, and re-layouts: 13.1 us -> 11.1 us
where the time goes in v1:
time: 390 us; the launch traced here: 389 us
  blocking collectives  121 us (31%)
  waiting for transfers between devices  116 us (30%)
  matrix products  61.8 us (16%)
  local copies, waits for them, and re-layouts  37.5 us (10%)
  starting transfers between devices  29.5 us (8%)
  between operations  17.2 us (4%)
  other arithmetic  6.85 us (2%)
    unnamed x2, blocking collectives  121 us
    reduce_scatter x1, waiting for transfers between devices, local(): lax.psum_scatter(summed.reshape(lax.axis_size('shard') * slots_dev, sourc...  87.8 us
    dot_general x1, matrix products, local(): lax.dot_general(value_part, value_local, contract, preferred_element_type...  11.4 us
    unnamed x44, local copies, waits for them, and re-layouts  11.1 us
    all_to_all x1, waiting for transfers between devices, local(): lax.all_to_all(query_split, 'shard', split_axis=2, concat_axis=0, tiled=T...  9.91 us
    all_gather x1, waiting for transfers between devices, local(): lax.all_gather(memory, 'lang', axis=0, tiled=True)  9.03 us
    dot_general x1, matrix products, local(): lax.dot_general(key_part, key_local, contract, preferred_element_type=jnp...  8.08 us
    all_to_all x1, waiting for transfers between devices, local(): lax.all_to_all(outgoing[1], 'shard', split_axis=0, concat_axis=2, tiled=T...  8.01 us
  transfers between devices with their start and end apart: 8, of which 4 were waited for; matrix products, arithmetic and copies ran while one was open for 18% of the time, Pallas kernels for 0%

profile of v1, /device:TPU:32, one launch (start us, length us, event | category | flops | bytes accessed | tf_op | source)
XLA Modules:
  0.0 389.3 jit_solution(6256275802189559168)
XLA Ops:
  7.2 0.0 copy-start
  7.2 0.0 all-gather.3.cloned.1.call-start
  7.2 0.7 all-gather.3.cloned.1.call-update
  7.9 3.1 copy.52
  11.1 2.7 copy.53
  13.8 7.5 %all-to-all-start.3 = ((bf16[2,128,32,128]{3,1,0,2:T(8,128)(2,1)}), bf16[2,128,32,128]{3,1,0,2:T(8,128)(2,1)S(1)}, u32[]{:S(2)}, u32[]{:S(2)}) async-start(bf16[2,128,32,128]{3,1,0,2:T(8,128)(2,1)} %copy.53), calls=%async_computation.3 | async-start | bytes 4194304 | tf_op jit(solution)/shard_map/all_to_all | solution.py:101
  23.2 0.6 dynamic-slice
  23.8 0.8 dynamic-update-slice
  24.6 0.8 dynamic-update-slice.3
  25.3 0.8 dynamic-update-slice.1
  26.1 15.3 %all-reduce.6 = (s32[8]{0:T(128)S(1)}, s32[8]{0:T(128)S(1)}, s32[8]{0:T(128)S(1)}) all-reduce(s32[8]{0:T(128)S(1)} %dynamic-update-slice.3, s32[8]{0:T(128)S(1)} %dynamic-update-slice, s32[8]{0:T(128)S(1)} %dynamic-update-slice.1), channel_id=1, replica_groups=mesh['lang'=8,'shard'=32] {'lang'}, use_global_device_ids=true, to_apply=%add.3 | all-reduce | flops 24 | bytes 192
  41.4 0.2 select_reduce_fusion
  41.6 9.0 %all-gather.3.cloned.1.call-done = bf16[8,16,4096]{2,1,0:T(8,128)(2,1)} async-done(((bf16[1,16,4096]{2,1,0:T(8,128)(2,1)}), bf16[8,16,4096]{2,1,0:T(8,128)(2,1)}) %all-gather.3.cloned.1.call-update) | async-done | bytes 1048592 | tf_op jit(solution)/shard_map/all_gather | solution.py:54
  50.6 2.5 convolution_convert_fusion.2
  53.1 0.1 copy.47
  53.3 0.0 copy-start.2
  53.3 4.3 %stack.2 = bf16[32,2,16,4096]{3,2,1,0:T(8,128)(2,1)} broadcast(bf16[2,16,4096]{2,1,0:T(8,128)(2,1)S(1)} %copy.47), dimensions={1,2,3} | broadcast | bytes 8650752 | tf_op jit(solution)/shard_map/stack | solution.py:78
  57.6 7.4 %all-to-all-start = ((bf16[32,2,16,4096]{3,2,1,0:T(8,128)(2,1)}), bf16[32,2,16,4096]{3,2,1,0:T(8,128)(2,1)}, u32[]{:S(2)}, u32[]{:S(2)}) async-start(bf16[32,2,16,4096]{3,2,1,0:T(8,128)(2,1)} %stack.2), calls=%async_computation | async-start | bytes 16777216 | tf_op jit(solution)/shard_map/all_to_all | solution.py:78
  65.0 0.6 dynamic-slice.2
  65.5 2.1 copy.56
  67.6 2.1 copy.49
  70.4 0.1 select_reduce_fusion.1
  70.6 0.2 dynamic-update-slice.2
  70.8 0.2 dynamic-update-slice.4
  71.0 105.6 %all-reduce.5 = (s32[64]{0:T(128)S(1)}, s32[64]{0:T(128)S(1)}) all-reduce(s32[64]{0:T(128)S(1)} %dynamic-update-slice.2, s32[64]{0:T(128)S(1)} %dynamic-update-slice.4), channel_id=1, replica_groups=mesh['lang'=8,'shard'=32] {'shard'}, use_global_device_ids=true, to_apply=%add.2 | all-reduce | flops 128 | bytes 1024
  176.6 0.1 iota_compare_fusion.1
  176.7 5.1 %all-to-all-start.1 = ((bf16[2,128,32,128]{3,1,0,2:T(8,128)(2,1)}), bf16[2,128,32,128]{3,1,0,2:T(8,128)(2,1)S(1)}, u32[]{:S(2)}, u32[]{:S(2)}) async-start(bf16[2,128,32,128]{3,1,0,2:T(8,128)(2,1)} %copy.49), calls=%async_computation.1 | async-start | bytes 4194304 | tf_op jit(solution)/shard_map/all_to_all | solution.py:100
  181.7 0.0 reduce-scatter.2.cloned.1.call-start
  181.8 0.1 iota_compare_fusion
  181.9 4.5 %bitcast_select_fusion.1 = bf16[64,128,128]{2,1,0:T(8,128)(2,1)} fusion(bf16[2,128,32,128]{3,1,0,2:T(8,128)(2,1)} %copy-done.2, pred[64,128]{1,0:T(8,128)(4,1)S(1)} %iota_compare_fusion.1), kind=kLoop, calls=%fused_computation.10 | loop fusion | flops 1048576 | bytes 4202496 | tf_op jit(solution)/shard_map/jit(_where)/select_n | solution.py:29
  186.4 6.3 %convolution_convert_fusion.4 = bf16[1024,128]{0,1:T(8,128)(2,1)S(1)} fusion(bf16[1024,4096]{1,0:T(8,128)(2,1)} %bitcast.3, bf16[1,4096,128]{2,1,0:T(8,128)(2,1)S(1)} %copy-done.3), kind=kOutput, calls=%fused_computation.20 | convolution fusion | flops 1073872896 | bytes 9699328 | tf_op jit(solution)/shard_map/dot_general | solution.py:84
  192.7 6.3 %convolution_convert_fusion.5 = bf16[1024,128]{0,1:T(8,128)(2,1)S(1)} fusion(bf16[1024,4096]{1,0:T(8,128)(2,1)} %bitcast.3, bf16[1,4096,128]{2,1,0:T(8,128)(2,1)S(1)} %copy-done), kind=kOutput, calls=%fused_computation.21 | convolution fusion | flops 1073872896 | bytes 9699328 | tf_op jit(solution)/shard_map/dot_general | solution.py:81
  198.9 0.8 pad_maximum_fusion
  199.8 2.0 copy.48
  201.8 9.9 %all-to-all-done.1 = bf16[2,128,32,128]{3,1,0,2:T(8,128)(2,1)S(1)} async-done(((bf16[2,128,32,128]{3,1,0,2:T(8,128)(2,1)}), bf16[2,128,32,128]{3,1,0,2:T(8,128)(2,1)S(1)}, u32[]{:S(2)}, u32[]{:S(2)}) %all-to-all-start.1) | async-done | bytes 2097184 | tf_op jit(solution)/shard_map/all_to_all | solution.py:100
  211.7 2.1 fusion.9
  213.9 0.8 copy-done.7
  214.7 0.9 fusion.26
  215.6 3.3 convolution_convert_fusion.3
  218.9 3.0 multiply_reduce_fusion
  221.9 0.0 copy-done.5
  221.9 0.1 multiply_convert_fusion.1
  222.0 0.7 fusion.10
  222.7 8.1 %fusion.13 = f32[1024,4096]{1,0:T(8,128)} fusion(bf16[1024,128]{1,0:T(8,128)(2,1)S(1)} %bitcast.112, bf16[1,4096,128]{2,1,0:T(8,128)(2,1)S(1)} %copy-done), kind=kOutput, calls=%fused_computation.25 | convolution fusion | flops 1073741824 | bytes 18087936 | tf_op jit(solution)/shard_map/dot_general | solution.py:124
  230.8 11.4 %add_convert_fusion = bf16[1024,4096]{1,0:T(8,128)(2,1)} fusion(f32[1024,4096]{1,0:T(8,128)} %fusion.13, bf16[1024,128]{1,0:T(8,128)(2,1)S(1)} %bitcast.114, bf16[1,4096,128]{2,1,0:T(8,128)(2,1)S(1)} %copy-done.4), kind=kOutput, calls=%fused_computation.1 | convolution fusion | flops 1082130432 | bytes 26476544 | tf_op jit(solution)/shard_map/dot_general | solution.py:125
  242.2 0.0 reduce-scatter.2.cloned.1.call-update
  242.2 1.0 copy-done.6
  243.2 0.2 copy-done.8
  243.4 2.4 fusion.5
  245.8 4.0 %all-to-all-start.2 = ((bf16[64,128,1,128]{1,3,2,0:T(8,128)(2,1)}), bf16[64,128,1,128]{1,3,2,0:T(8,128)(2,1)S(1)}, u32[]{:S(2)}, u32[]{:S(2)}) async-start(bf16[64,128,1,128]{1,3,2,0:T(8,128)(2,1)} %fusion.5), calls=%async_computation.2 | async-start | bytes 4194304 | tf_op jit(solution)/shard_map/all_to_all | solution.py:114
  249.8 0.0 all-gather.5.cloned.1.call-start
  249.9 87.8 %reduce-scatter.2.cloned.1.call-done = bf16[2,16,4096]{2,1,0:T(8,128)(2,1)} async-done(((bf16[64,16,4096]{2,1,0:T(8,128)(2,1)}), bf16[2,16,4096]{2,1,0:T(8,128)(2,1)}) %reduce-scatter.2.cloned.1.call-update) | async-done | bytes 262160 | tf_op jit(solution)/shard_map/reduce_scatter | solution.py:128
  337.7 0.0 all-gather.5.cloned.1.call-update
  337.8 2.1 fusion.4
  339.9 5.5 %all-to-all-start.4 = ((bf16[64,128,1,128]{1,3,2,0:T(8,128)(2,1)}), bf16[64,128,1,128]{1,3,2,0:T(8,128)(2,1)}, u32[]{:S(2)}, u32[]{:S(2)}) async-start(bf16[64,128,1,128]{1,3,2,0:T(8,128)(2,1)} %fusion.4), calls=%async_computation.4 | async-start | bytes 4194304 | tf_op jit(solution)/shard_map/all_to_all | solution.py:115
  345.4 0.6 dynamic_slice.6
  346.6 6.8 %fusion.1 = bf16[1,4096,128]{2,1,0:T(8,128)(2,1)} fusion(bf16[1024,4096]{1,0:T(8,128)(2,1)} %bitcast.3, bf16[1024,128]{1,0:T(8,128)(2,1)S(1)} %bitcast.113), kind=kOutput, calls=%fused_computation.4 | convolution fusion | flops 1074266112 | bytes 9699328 | tf_op jit(solution)/shard_map/dot_general | solution.py:138
  353.4 6.8 %fusion.2 = bf16[1,4096,128]{2,1,0:T(8,128)(2,1)} fusion(bf16[1024,4096]{1,0:T(8,128)(2,1)} %bitcast.3, bf16[1024,128]{1,0:T(8,128)(2,1)S(1)} %bitcast.115), kind=kOutput, calls=%fused_computation.5 | convolution fusion | flops 1074266112 | bytes 9699328 | tf_op jit(solution)/shard_map/dot_general | solution.py:144
  360.3 2.9 copy.51
  363.1 4.2 %reshape.148 = bf16[1,2,128,4096]{3,2,1,0:T(8,128)(2,1)} reshape(bf16[2,128,32,1,128]{4,2,1,0,3:T(8,128)(2,1)} %copy.51) | data formatting | bytes 4194304 | tf_op jit(solution)/shard_map/reshape | solution.py:117
  367.3 8.0 %all-to-all-done.4 = bf16[64,128,1,128]{1,3,2,0:T(8,128)(2,1)} async-done(((bf16[64,128,1,128]{1,3,2,0:T(8,128)(2,1)}), bf16[64,128,1,128]{1,3,2,0:T(8,128)(2,1)}, u32[]{:S(2)}, u32[]{:S(2)}) %all-to-all-start.4) | async-done | bytes 2097184 | tf_op jit(solution)/shard_map/all_to_all | solution.py:115
  375.3 3.6 copy.55
  378.9 2.3 reshape.149
  381.2 1.6 constant_dynamic-slice_fusion
  (35 shorter events, 0.1 us)
Async XLA Ops:
  7.2 185.5 %copy-start = (bf16[1,4096,128]{2,1,0:T(8,128)(2,1)S(1)}, bf16[1,4096,128]{2,1,0:T(8,128)(2,1)}, u32[]{:S(2)}) copy-start(bf16[1,4096,128]{2,1,0:T(8,128)(2,1)} %param.13) | copy-start | bytes 3145732
  7.2 43.4 %all-gather.3.cloned.1.call-start = ((), (), s32[]{:S(2)}) async-start(), calls=%async_computation.6 | async-start | bytes 1179648 | tf_op jit(solution)/shard_map/all_gather | solution.py:54
  13.8 9.4 %copy-start.14 = (u32[256]{0:T(256)S(1)}, u32[256]{0:T(256)}, u32[]{:S(2)}) copy-start(u32[256]{0:T(256)} %constant.40) | copy-start | bytes 3076
  13.8 39.5 %all-to-all-start.3 = ((bf16[2,128,32,128]{3,1,0,2:T(8,128)(2,1)}), bf16[2,128,32,128]{3,1,0,2:T(8,128)(2,1)S(1)}, u32[]{:S(2)}, u32[]{:S(2)}) async-start(bf16[2,128,32,128]{3,1,0,2:T(8,128)(2,1)} %copy.53), calls=%async_computation.3 | async-start | bytes 4194304 | tf_op jit(solution)/shard_map/all_to_all | solution.py:101
  53.3 4.3 %copy-start.2 = (bf16[2,128,32,128]{3,1,0,2:T(8,128)(2,1)}, bf16[2,128,32,128]{3,1,0,2:T(8,128)(2,1)S(1)}, u32[]{:S(2)}) copy-start(bf16[2,128,32,128]{3,1,0,2:T(8,128)(2,1)S(1)} %all-to-all-done.3) | copy-start | bytes 6291460
  57.6 7.4 %copy-start.13 = (u32[256]{0:T(256)S(1)}, u32[256]{0:T(256)}, u32[]{:S(2)}) copy-start(u32[256]{0:T(256)} %constant.50) | copy-start | bytes 3076
  57.6 119.1 %all-to-all-start = ((bf16[32,2,16,4096]{3,2,1,0:T(8,128)(2,1)}), bf16[32,2,16,4096]{3,2,1,0:T(8,128)(2,1)}, u32[]{:S(2)}, u32[]{:S(2)}) async-start(bf16[32,2,16,4096]{3,2,1,0:T(8,128)(2,1)} %stack.2), calls=%async_computation | async-start | bytes 16777216 | tf_op jit(solution)/shard_map/all_to_all | solution.py:78
  176.7 35.1 %all-to-all-start.1 = ((bf16[2,128,32,128]{3,1,0,2:T(8,128)(2,1)}), bf16[2,128,32,128]{3,1,0,2:T(8,128)(2,1)S(1)}, u32[]{:S(2)}, u32[]{:S(2)}) async-start(bf16[2,128,32,128]{3,1,0,2:T(8,128)(2,1)} %copy.49), calls=%async_computation.1 | async-start | bytes 4194304 | tf_op jit(solution)/shard_map/all_to_all | solution.py:100
  181.7 156.0 %reduce-scatter.2.cloned.1.call-start = ((), (), s32[]{:S(2)}) async-start(), calls=%async_computation.7 | async-start | bytes 8650752 | tf_op jit(solution)/shard_map/reduce_scatter | solution.py:128
  181.9 4.5 %copy-start.3 = (bf16[1,4096,128]{2,1,0:T(8,128)(2,1)S(1)}, bf16[1,4096,128]{2,1,0:T(8,128)(2,1)}, u32[]{:S(2)}) copy-start(bf16[1,4096,128]{2,1,0:T(8,128)(2,1)} %param.14) | copy-start | bytes 3145732
  213.9 0.8 copy-start.7
  218.9 3.0 copy-start.5
  222.7 8.1 %copy-start.9 = (bf16[64,16,128]{2,1,0:T(8,128)(2,1)}, bf16[64,16,128]{2,1,0:T(8,128)(2,1)S(1)}, u32[]{:S(2)}) copy-start(bf16[64,16,128]{2,1,0:T(8,128)(2,1)S(1)} %fusion.10) | copy-start | bytes 786436
  222.7 8.1 %copy-start.4 = (bf16[1,4096,128]{2,1,0:T(8,128)(2,1)S(1)}, bf16[1,4096,128]{2,1,0:T(8,128)(2,1)}, u32[]{:S(2)}) copy-start(bf16[1,4096,128]{2,1,0:T(8,128)(2,1)} %param.14) | copy-start | bytes 3145732
  222.7 8.1 %copy-start.11 = (bf16[64,128,16]{1,2,0:T(8,128)(2,1)S(1)}, bf16[64,128,16]{1,2,0:T(8,128)(2,1)}, u32[]{:S(2)}) copy-start(bf16[64,128,16]{1,2,0:T(8,128)(2,1)} %convolution_convert_fusion.3) | copy-start | bytes 786436
  242.2 1.0 copy-start.6
  242.2 1.2 copy-start.8
  245.8 94.0 %all-to-all-start.2 = ((bf16[64,128,1,128]{1,3,2,0:T(8,128)(2,1)}), bf16[64,128,1,128]{1,3,2,0:T(8,128)(2,1)S(1)}, u32[]{:S(2)}, u32[]{:S(2)}) async-start(bf16[64,128,1,128]{1,3,2,0:T(8,128)(2,1)} %fusion.5), calls=%async_computation.2 | async-start | bytes 4194304 | tf_op jit(solution)/shard_map/all_to_all | solution.py:114
  249.8 131.3 %all-gather.5.cloned.1.call-start = ((), (), s32[]{:S(2)}) async-start(), calls=%async_computation.8 | async-start | bytes 2359296 | tf_op jit(solution)/shard_map/all_gather | solution.py:150
  339.9 6.7 %copy-start.10 = (bf16[64,16,128]{2,1,0:T(8,128)(2,1)S(1)}, bf16[64,16,128]{2,1,0:T(8,128)(2,1)}, u32[]{:S(2)}) copy-start(bf16[64,16,128]{2,1,0:T(8,128)(2,1)} %copy-done.9) | copy-start | bytes 786436
  339.9 35.4 %all-to-all-start.4 = ((bf16[64,128,1,128]{1,3,2,0:T(8,128)(2,1)}), bf16[64,128,1,128]{1,3,2,0:T(8,128)(2,1)}, u32[]{:S(2)}, u32[]{:S(2)}) async-start(bf16[64,128,1,128]{1,3,2,0:T(8,128)(2,1)} %fusion.4), calls=%async_computation.4 | async-start | bytes 4194304 | tf_op jit(solution)/shard_map/all_to_all | solution.py:115
  346.6 6.8 %copy-start.12 = (bf16[64,128,16]{1,2,0:T(8,128)(2,1)S(1)}, bf16[64,128,16]{1,2,0:T(8,128)(2,1)}, u32[]{:S(2)}) copy-start(bf16[64,128,16]{1,2,0:T(8,128)(2,1)} %convolution_convert_fusion.3) | copy-start | bytes 786436
  375.3 7.4 %copy-start.1 = (bf16[1,4096,128]{2,1,0:T(8,128)(2,1)S(1)}, bf16[1,4096,128]{2,1,0:T(8,128)(2,1)}, u32[]{:S(2)}) copy-start(bf16[1,4096,128]{2,1,0:T(8,128)(2,1)} %param.13) | copy-start | bytes 3145732
Sparse Core Ops, SparseCore 0:
  9.8 40.7 all-gather.2
  242.4 95.3 reduce-scatter.1
  339.7 40.2 all-gather.4
